TPU v7x, 512 devices: a whole 4x4x16 slice. The times are simulated.
512 devices in a mesh: blk: 32 (over x, y, core), uly: 16 (over z).
Axes of the slice: x: 4, y: 4, z: 16, core: 2. Of those that a mesh axis runs over, the one named last changes fastest.
Arguments:
- queries: bfloat16 [8192, 6144], P(('blk', 'uly')), may hold values from -120 to 120
- keys: bfloat16 [8192, 6144], P(('blk', 'uly')), may hold values from -6 to 6
- values: bfloat16 [8192, 6144], P(('blk', 'uly')), may hold values from -6 to 6
- window_mask: int32 [128, 27], P('blk'), may hold values from 0 to 1, as said below
- valid_count: int32 [128], P('blk'), may hold values from 2 to 64, as said below
Outputs:
- attended: bfloat16 [8192, 6144], P(('blk', 'uly'))
Inputs may be any that keep to these rules, and one draw needn't show every extreme that they name: `window_mask`: entry o of a tile's row is 1 only if the tile at offset (o // 9 - 1, o // 3 % 3 - 1, o % 3 - 1) lies inside the grid; entry 13 (the tile itself) is always 1. `valid_count`: some tile has all 64 tokens live.
All inputs are finite; a program needn't handle non-finite values.
Results may differ from a plain program's by a relative error of at most 0.0033.
Values may be sent and summed in bfloat16 or wider, within the bound.
A program may use at most 64 MiB of HBM per device.

v0:
```python
import math

import jax
import jax.numpy as jnp
from jax import lax
from jax.sharding import PartitionSpec as P

HDIM = 128
TILE = 64
TFRAMES = 1
TH_DEV = 2
TW_DEV = 2
ROWB = 4


def for_sending(shard):

    def short(part):
        return part.astype(jnp.bfloat16) if part.dtype == jnp.float32 else part

    return jax.tree.map(short, shard)


def shifted(shard, axis, by):
    peers = lax.axis_size(axis)
    pairs = [(i, i + by) for i in range(peers) if 0 <= i + by < peers]
    return lax.ppermute(shard, axis, pairs)


def extend_direct(pieces, col_blocks):
    place = lax.axis_index("blk")
    column = place % col_blocks
    row_block = place // col_blocks
    row_blocks = lax.axis_size("blk") // col_blocks
    received = {}
    for row_move in (-1, 0, 1):
        for col_move in (-1, 0, 1):
            if row_move == 0 and col_move == 0:
                continue
            row_part = (
                slice(0, 1) if row_move == 1 else slice(-1, None) if row_move == -1 else slice(None)
            )
            col_part = (
                slice(0, 1) if col_move == 1 else slice(-1, None) if col_move == -1 else slice(None)
            )
            edges = tuple((piece[:, row_part, col_part] for piece in pieces))
            arrived = jax.tree.map(
                lambda part, own: part.astype(own.dtype),
                shifted(for_sending(edges), "blk", -(row_move * col_blocks + col_move)),
                edges,
            )
            inside = (
                (column + col_move >= 0)
                & (column + col_move < col_blocks)
                & (row_block + row_move >= 0)
                & (row_block + row_move < row_blocks)
            )
            received[row_move, col_move] = tuple(
                (jnp.where(inside, got, jnp.zeros_like(got)) for got in arrived)
            )
    results = []
    for index in range(len(pieces)):
        bands = []
        for row_move in (-1, 0, 1):
            cells = [
                (
                    pieces[index]
                    if row_move == 0 and col_move == 0
                    else received[row_move, col_move][index]
                )
                for col_move in (-1, 0, 1)
            ]
            bands.append(jnp.concatenate(cells, axis=2))
        results.append(jnp.concatenate(bands, axis=1))
    return tuple(results)


def window_block(k_padded, v_padded, c_padded, window_live, offset_group):
    positions = jnp.arange(TILE, dtype=jnp.float32)
    key_parts, value_parts, live_parts = ([], [], [])
    for window_offset in offset_group:
        frame_step, row_step, column_step = (
            window_offset // 9,
            window_offset // 3 % 3,
            window_offset % 3,
        )
        key_parts.append(
            k_padded[
                frame_step : frame_step + TFRAMES,
                row_step : row_step + TH_DEV,
                column_step : column_step + TW_DEV,
            ]
        )
        value_parts.append(
            v_padded[
                frame_step : frame_step + TFRAMES,
                row_step : row_step + TH_DEV,
                column_step : column_step + TW_DEV,
            ]
        )
        count_tiles = c_padded[
            frame_step : frame_step + TFRAMES,
            row_step : row_step + TH_DEV,
            column_step : column_step + TW_DEV,
        ].astype(jnp.float32)
        live_parts.append(
            (positions[None, None, None, :] < count_tiles[..., None])
            & (window_live[..., window_offset : window_offset + 1] > 0)
        )
    return (key_parts[0], value_parts[0], live_parts[0])


def attend_block(q_rows, k_rows, v_rows, counts, window_live):
    head_count = q_rows.shape[1]
    tile_shape = (TFRAMES, TH_DEV, TW_DEV, TILE, head_count, HDIM)
    col_blocks = lax.axis_size("blk") // ROWB
    pieces = (k_rows.reshape(tile_shape), v_rows.reshape(tile_shape), counts)
    k_ext, v_ext, c_ext = extend_direct(pieces, col_blocks)
    spacing = ((1, 1), (0, 0), (0, 0), (0, 0), (0, 0), (0, 0))
    k_padded = jnp.pad(k_ext, spacing)
    v_padded = jnp.pad(v_ext, spacing)
    c_padded = jnp.pad(c_ext, ((1, 1), (0, 0), (0, 0)))
    q_tiles = q_rows.reshape(tile_shape)
    score_scale = 1.0 / math.sqrt(HDIM)
    offset_groups = [[window_offset] for window_offset in range(27)]

    def scores_of(key_block, live_block):
        raw_scores = (
            jnp.einsum(
                "fabqhd,fabkhd->fabhqk", q_tiles, key_block, preferred_element_type=jnp.float32
            )
            * score_scale
        )
        return jnp.where(live_block[:, :, :, None, None, :], raw_scores, -1e30)

    row_peak = jnp.full((TFRAMES, TH_DEV, TW_DEV, head_count, TILE), -1e30, jnp.float32)
    for offset_group in offset_groups:
        key_block, value_block, live_block = window_block(
            k_padded, v_padded, c_padded, window_live, offset_group
        )
        row_peak = jnp.maximum(row_peak, jnp.max(scores_of(key_block, live_block), axis=-1))
    row_total = jnp.zeros((TFRAMES, TH_DEV, TW_DEV, head_count, TILE), jnp.float32)
    summed = jnp.zeros(tile_shape, jnp.float32)
    for offset_group in offset_groups:
        key_block, value_block, live_block = window_block(
            k_padded, v_padded, c_padded, window_live, offset_group
        )
        exp_terms = jnp.where(
            live_block[:, :, :, None, None, :],
            jnp.exp(scores_of(key_block, live_block) - row_peak[..., None]),
            0.0,
        )
        row_total = row_total + jnp.sum(exp_terms, axis=-1)
        summed = summed + jnp.einsum(
            "fabhqk,fabkhd->fabqhd",
            exp_terms.astype(jnp.bfloat16),
            value_block,
            preferred_element_type=jnp.float32,
        )
    attended = (summed / jnp.swapaxes(row_total, 3, 4)[..., None]).astype(jnp.bfloat16)
    return attended.reshape(q_rows.shape[0], head_count, HDIM)


def on_device(queries, keys, values, window_mask, valid_count):
    token_rows = queries.shape[0]
    uly_count = lax.axis_size("uly")
    patch_tokens = token_rows * uly_count
    counts = valid_count.reshape(TFRAMES, TH_DEV, TW_DEV).astype(jnp.bfloat16)
    window_live = window_mask.reshape(TFRAMES, TH_DEV, TW_DEV, 27)
    q_local, k_local, v_local = (
        lax.all_to_all(queries, "uly", split_axis=1, concat_axis=0, tiled=True),
        lax.all_to_all(keys, "uly", split_axis=1, concat_axis=0, tiled=True),
        lax.all_to_all(values, "uly", split_axis=1, concat_axis=0, tiled=True),
    )
    head_count = q_local.shape[1] // HDIM
    shaped = (patch_tokens, head_count, HDIM)
    result = attend_block(
        q_local.reshape(shaped),
        k_local.reshape(shaped),
        v_local.reshape(shaped),
        counts,
        window_live,
    )
    return lax.all_to_all(
        result.reshape(patch_tokens, head_count * HDIM),
        "uly",
        split_axis=0,
        concat_axis=1,
        tiled=True,
    )


def solution(mesh):
    in_specs = (
        P(("blk", "uly"), None),
        P(("blk", "uly"), None),
        P(("blk", "uly"), None),
        P("blk", None),
        P("blk"),
    )
    out_specs = P(("blk", "uly"), None)
    return jax.shard_map(
        on_device, mesh=mesh, in_specs=in_specs, out_specs=out_specs, check_vma=False
    )
```

profile of v0, /device:TPU:25, one launch (start us, length us, event | category | flops | bytes accessed | tf_op | source)
XLA Modules:
  0.0 198.0 jit_solution(13021086066499228621)
XLA Ops:
  1.4 5.4 %collective-permute-start.5 = (bf16[1,1,1]{2,1,0:T(2,128)(2,1)}, bf16[1,1,1]{2,1,0:T(2,128)(2,1)}, u32[]{:S(2)}, u32[]{:S(2)}) collective-permute-start(bf16[1,1,1]{2,1,0:T(2,128)(2,1)} %get-tuple-element.50), channel_id=1, source_target_pairs={{0,144},{16,160},{32,176},{48,192},{64,208},{80,224},{96,240},{112... | collective-permute-start | bytes 14 | tf_op jit(solution)/shard_map/ppermute | solution.py:27
  6.8 1.9 collective-permute-start.7
  8.7 5.4 %collective-permute-start.15 = (bf16[1,1,1]{2,1,0:T(2,128)(2,1)}, bf16[1,1,1]{2,1,0:T(2,128)(2,1)}, u32[]{:S(2)}, u32[]{:S(2)}) collective-permute-start(bf16[1,1,1]{2,1,0:T(2,128)(2,1)} %get-tuple-element.52), channel_id=1, source_target_pairs={{112,0},{128,16},{144,32},{160,48},{176,64},{192,80},{208,96},{224... | collective-permute-start | bytes 14 | tf_op jit(solution)/shard_map/ppermute | solution.py:27
  14.2 1.3 collective-permute-start.17
  15.5 1.3 collective-permute-start.16
  16.8 1.6 copy.147
  18.4 14.9 %all-to-all-start.1 = ((bf16[16,16,384]{2,0,1:T(8,128)(2,1)}), bf16[16,16,384]{2,0,1:T(8,128)(2,1)S(1)}, u32[]{:S(2)}, u32[]{:S(2)}) async-start(bf16[16,16,384]{2,0,1:T(8,128)(2,1)} %bitcast.222), calls=%async_computation.1 | async-start | bytes 393216 | tf_op jit(solution)/shard_map/all_to_all | solution.py:172
  36.6 1.9 collective-permute-start.9
  39.2 5.8 %collective-permute-start.8 = (bf16[1,2,1]{2,1,0:T(2,128)(2,1)S(1)}, bf16[1,2,1]{2,1,0:T(2,128)(2,1)S(1)}, u32[]{:S(2)}, u32[]{:S(2)}) collective-permute-start(bf16[1,2,1]{2,1,0:T(2,128)(2,1)S(1)} %get-tuple-element.60), channel_id=1, source_target_pairs={{0,16},{16,32},{32,48},{48,64},{64,80},{80,96},{96,112},{112,128},... | collective-permute-start | bytes 20 | tf_op jit(solution)/shard_map/ppermute | solution.py:27
  45.6 4.6 %collective-permute-start.6 = (bf16[1,1,2]{2,1,0:T(2,128)(2,1)S(1)}, bf16[1,1,2]{2,1,0:T(2,128)(2,1)S(1)}, u32[]{:S(2)}, u32[]{:S(2)}) collective-permute-start(bf16[1,1,2]{2,1,0:T(2,128)(2,1)S(1)} %get-tuple-element.54), channel_id=1, source_target_pairs={{0,128},{16,144},{32,160},{48,176},{64,192},{80,208},{96,224},{112... | collective-permute-start | bytes 20 | tf_op jit(solution)/shard_map/ppermute | solution.py:27
  52.1 11.7 %all-to-all-start = ((bf16[16,16,384]{2,0,1:T(8,128)(2,1)}), bf16[16,16,384]{2,0,1:T(8,128)(2,1)S(1)}, u32[]{:S(2)}, u32[]{:S(2)}) async-start(bf16[16,16,384]{2,0,1:T(8,128)(2,1)} %bitcast.223), calls=%async_computation | async-start | bytes 393216 | tf_op jit(solution)/shard_map/all_to_all | solution.py:173
  64.2 13.9 %all-to-all-done = bf16[16,16,384]{2,0,1:T(8,128)(2,1)S(1)} async-done(((bf16[16,16,384]{2,0,1:T(8,128)(2,1)}), bf16[16,16,384]{2,0,1:T(8,128)(2,1)S(1)}, u32[]{:S(2)}, u32[]{:S(2)}) %all-to-all-start) | async-done | bytes 196640 | tf_op jit(solution)/shard_map/all_to_all | solution.py:173
  78.1 3.8 %all-to-all-start.2 = ((bf16[16,16,384]{2,0,1:T(8,128)(2,1)}), bf16[16,16,384]{2,0,1:T(8,128)(2,1)S(1)}, u32[]{:S(2)}, u32[]{:S(2)}) async-start(bf16[16,16,384]{2,0,1:T(8,128)(2,1)} %bitcast.221), calls=%async_computation.2 | async-start | bytes 393216 | tf_op jit(solution)/shard_map/all_to_all | solution.py:171
  83.4 1.9 collective-permute-start.14
  85.4 6.7 %collective-permute-start.13 = (bf16[1,2,1,64,3,128]{5,3,4,2,1,0:T(8,128)(2,1)S(1)}, bf16[1,2,1,64,3,128]{5,3,4,2,1,0:T(8,128)(2,1)S(1)}, u32[]{:S(2)}, u32[]{:S(2)}) collective-permute-start(bf16[1,2,1,64,3,128]{5,3,4,2,1,0:T(8,128)(2,1)S(1)} %get-tuple-element.40), channel_id=1, source_target_pairs={{0,16},{16,32},{32,48},{48,64},{64,80},{80,96},{96,112},{112,128},... | collective-permute-start | bytes 294920 | tf_op jit(solution)/shard_map/ppermute | solution.py:27
  92.1 3.6 %collective-permute-start.11 = (bf16[1,1,2,64,3,128]{5,3,4,2,1,0:T(8,128)(2,1)S(1)}, bf16[1,1,2,64,3,128]{5,3,4,2,1,0:T(8,128)(2,1)S(1)}, u32[]{:S(2)}, u32[]{:S(2)}) collective-permute-start(bf16[1,1,2,64,3,128]{5,3,4,2,1,0:T(8,128)(2,1)S(1)} %get-tuple-element.36), channel_id=1, source_target_pairs={{0,128},{16,144},{32,160},{48,176},{64,192},{80,208},{96,224},{112... | collective-permute-start | bytes 294920 | tf_op jit(solution)/shard_map/ppermute | solution.py:27
  95.8 1.9 collective-permute-start.18
  98.3 2.9 %collective-permute-done.18 = bf16[1,1,1,64,3,128]{5,3,4,2,1,0:T(8,128)(2,1)S(1)} collective-permute-done((bf16[1,1,1,64,3,128]{5,3,4,2,1,0:T(8,128)(2,1)S(1)}, bf16[1,1,1,64,3,128]{5,3,4,2,1,0:T(8,128)(2,1)S(1)}, u32[]{:S(2)}, u32[]{:S(2)}) %collective-permute-start.18) | collective-permute-done | bytes 49184 | tf_op jit(solution)/shard_map/ppermute | solution.py:27
  101.2 1.9 collective-permute-start.12
  103.1 4.7 %collective-permute-done.12 = bf16[1,1,1,64,3,128]{5,3,4,2,1,0:T(8,128)(2,1)S(1)} collective-permute-done((bf16[1,1,1,64,3,128]{5,3,4,2,1,0:T(8,128)(2,1)S(1)}, bf16[1,1,1,64,3,128]{5,3,4,2,1,0:T(8,128)(2,1)S(1)}, u32[]{:S(2)}, u32[]{:S(2)}) %collective-permute-start.12) | collective-permute-done | bytes 49184 | tf_op jit(solution)/shard_map/ppermute | solution.py:27
  107.8 4.7 %collective-permute-start.10 = (bf16[1,1,1,64,3,128]{5,3,4,2,1,0:T(8,128)(2,1)S(1)}, bf16[1,1,1,64,3,128]{5,3,4,2,1,0:T(8,128)(2,1)S(1)}, u32[]{:S(2)}, u32[]{:S(2)}) collective-permute-start(bf16[1,1,1,64,3,128]{5,3,4,2,1,0:T(8,128)(2,1)S(1)} %get-tuple-element.32), channel_id=1, source_target_pairs={{0,144},{16,160},{32,176},{48,192},{64,208},{80,224},{96,240},{112... | collective-permute-start | bytes 147464 | tf_op jit(solution)/shard_map/ppermute | solution.py:27
  115.0 8.3 %collective-permute-done.20 = bf16[1,1,1,64,3,128]{5,3,4,2,1,0:T(8,128)(2,1)S(1)} collective-permute-done((bf16[1,1,1,64,3,128]{5,3,4,2,1,0:T(8,128)(2,1)S(1)}, bf16[1,1,1,64,3,128]{5,3,4,2,1,0:T(8,128)(2,1)S(1)}, u32[]{:S(2)}, u32[]{:S(2)}) %collective-permute-start.20) | collective-permute-done | bytes 49184 | tf_op jit(solution)/shard_map/ppermute | solution.py:27
  123.3 1.9 collective-permute-start.21
  125.2 3.5 %collective-permute-done.21 = bf16[1,1,1,64,3,128]{5,3,4,2,1,0:T(8,128)(2,1)S(1)} collective-permute-done((bf16[1,1,1,64,3,128]{5,3,4,2,1,0:T(8,128)(2,1)S(1)}, bf16[1,1,1,64,3,128]{5,3,4,2,1,0:T(8,128)(2,1)S(1)}, u32[]{:S(2)}, u32[]{:S(2)}) %collective-permute-start.21) | collective-permute-done | bytes 49184 | tf_op jit(solution)/shard_map/ppermute | solution.py:27
  128.7 1.9 collective-permute-start.2
  130.6 4.7 %collective-permute-done.2 = bf16[1,1,1,64,3,128]{5,3,4,2,1,0:T(8,128)(2,1)S(1)} collective-permute-done((bf16[1,1,1,64,3,128]{5,3,4,2,1,0:T(8,128)(2,1)S(1)}, bf16[1,1,1,64,3,128]{5,3,4,2,1,0:T(8,128)(2,1)S(1)}, u32[]{:S(2)}, u32[]{:S(2)}) %collective-permute-start.2) | collective-permute-done | bytes 49184 | tf_op jit(solution)/shard_map/ppermute | solution.py:27
  135.3 4.1 %collective-permute-start = (bf16[1,1,1,64,3,128]{5,3,4,2,1,0:T(8,128)(2,1)S(1)}, bf16[1,1,1,64,3,128]{5,3,4,2,1,0:T(8,128)(2,1)S(1)}, u32[]{:S(2)}, u32[]{:S(2)}) collective-permute-start(bf16[1,1,1,64,3,128]{5,3,4,2,1,0:T(8,128)(2,1)S(1)} %get-tuple-element.26), channel_id=1, source_target_pairs={{0,144},{16,160},{32,176},{48,192},{64,208},{80,224},{96,240},{112... | collective-permute-start | bytes 147464 | tf_op jit(solution)/shard_map/ppermute | solution.py:27
  141.9 8.3 %collective-permute-done.23 = bf16[1,1,1,64,3,128]{5,3,4,2,1,0:T(8,128)(2,1)S(1)} collective-permute-done((bf16[1,1,1,64,3,128]{5,3,4,2,1,0:T(8,128)(2,1)S(1)}, bf16[1,1,1,64,3,128]{5,3,4,2,1,0:T(8,128)(2,1)S(1)}, u32[]{:S(2)}, u32[]{:S(2)}) %collective-permute-start.23) | collective-permute-done | bytes 49184 | tf_op jit(solution)/shard_map/ppermute | solution.py:27
  151.5 1.9 collective-permute-start.4
  153.4 5.8 %collective-permute-start.3 = (bf16[1,2,1,64,3,128]{5,3,4,2,1,0:T(8,128)(2,1)S(1)}, bf16[1,2,1,64,3,128]{5,3,4,2,1,0:T(8,128)(2,1)S(1)}, u32[]{:S(2)}, u32[]{:S(2)}) collective-permute-start(bf16[1,2,1,64,3,128]{5,3,4,2,1,0:T(8,128)(2,1)S(1)} %get-tuple-element.38), channel_id=1, source_target_pairs={{0,16},{16,32},{32,48},{48,64},{64,80},{80,96},{96,112},{112,128},... | collective-permute-start | bytes 294920 | tf_op jit(solution)/shard_map/ppermute | solution.py:27
  159.2 4.0 %collective-permute-start.1 = (bf16[1,1,2,64,3,128]{5,3,4,2,1,0:T(8,128)(2,1)S(1)}, bf16[1,1,2,64,3,128]{5,3,4,2,1,0:T(8,128)(2,1)S(1)}, u32[]{:S(2)}, u32[]{:S(2)}) collective-permute-start(bf16[1,1,2,64,3,128]{5,3,4,2,1,0:T(8,128)(2,1)S(1)} %get-tuple-element.30), channel_id=1, source_target_pairs={{0,128},{16,144},{32,160},{48,176},{64,192},{80,208},{96,224},{112... | collective-permute-start | bytes 294920 | tf_op jit(solution)/shard_map/ppermute | solution.py:27
  170.7 26.6 %all_to_all.67 = bf16[16,16,384]{2,1,0:T(8,128)(2,1)S(1)} all-to-all(bf16[16,16,384]{2,1,0:T(8,128)(2,1)S(1)} %all_to_all.59), channel_id=1, replica_groups=mesh['blk'=32,'uly'=16] {'uly'}, dimensions={0} | all-to-all | bytes 393216 | tf_op jit(solution)/shard_map/all_to_all | solution.py:184
  (114 shorter events, 21.8 us)
Async XLA Ops:
  1.4 35.2 %collective-permute-start.5 = (bf16[1,1,1]{2,1,0:T(2,128)(2,1)}, bf16[1,1,1]{2,1,0:T(2,128)(2,1)}, u32[]{:S(2)}, u32[]{:S(2)}) collective-permute-start(bf16[1,1,1]{2,1,0:T(2,128)(2,1)} %get-tuple-element.50), channel_id=1, source_target_pairs={{0,144},{16,160},{32,176},{48,192},{64,208},{80,224},{96,240},{112... | collective-permute-start | bytes 14 | tf_op jit(solution)/shard_map/ppermute | solution.py:27
  6.8 32.3 %collective-permute-start.7 = (bf16[1,1,1]{2,1,0:T(2,128)(2,1)}, bf16[1,1,1]{2,1,0:T(2,128)(2,1)}, u32[]{:S(2)}, u32[]{:S(2)}) collective-permute-start(bf16[1,1,1]{2,1,0:T(2,128)(2,1)} %get-tuple-element.53), channel_id=1, source_target_pairs={{0,112},{16,128},{32,144},{48,160},{64,176},{80,192},{96,208},{112... | collective-permute-start | bytes 14 | tf_op jit(solution)/shard_map/ppermute | solution.py:27
  8.7 36.8 %collective-permute-start.15 = (bf16[1,1,1]{2,1,0:T(2,128)(2,1)}, bf16[1,1,1]{2,1,0:T(2,128)(2,1)}, u32[]{:S(2)}, u32[]{:S(2)}) collective-permute-start(bf16[1,1,1]{2,1,0:T(2,128)(2,1)} %get-tuple-element.52), channel_id=1, source_target_pairs={{112,0},{128,16},{144,32},{160,48},{176,64},{192,80},{208,96},{224... | collective-permute-start | bytes 14 | tf_op jit(solution)/shard_map/ppermute | solution.py:27
  14.2 36.6 %collective-permute-start.17 = (bf16[1,1,1]{2,1,0:T(2,128)(2,1)}, bf16[1,1,1]{2,1,0:T(2,128)(2,1)}, u32[]{:S(2)}, u32[]{:S(2)}) collective-permute-start(bf16[1,1,1]{2,1,0:T(2,128)(2,1)} %get-tuple-element.51), channel_id=1, source_target_pairs={{144,0},{160,16},{176,32},{192,48},{208,64},{224,80},{240,96},{256... | collective-permute-start | bytes 14 | tf_op jit(solution)/shard_map/ppermute | solution.py:27
  15.5 36.1 %collective-permute-start.16 = (bf16[1,1,2]{2,1,0:T(2,128)(2,1)S(1)}, bf16[1,1,2]{2,1,0:T(2,128)(2,1)S(1)}, u32[]{:S(2)}, u32[]{:S(2)}) collective-permute-start(bf16[1,1,2]{2,1,0:T(2,128)(2,1)S(1)} %get-tuple-element.55), channel_id=1, source_target_pairs={{128,0},{144,16},{160,32},{176,48},{192,64},{208,80},{224,96},{240... | collective-permute-start | bytes 20 | tf_op jit(solution)/shard_map/ppermute | solution.py:27
  18.4 33.7 %all-to-all-start.1 = ((bf16[16,16,384]{2,0,1:T(8,128)(2,1)}), bf16[16,16,384]{2,0,1:T(8,128)(2,1)S(1)}, u32[]{:S(2)}, u32[]{:S(2)}) async-start(bf16[16,16,384]{2,0,1:T(8,128)(2,1)} %bitcast.222), calls=%async_computation.1 | async-start | bytes 393216 | tf_op jit(solution)/shard_map/all_to_all | solution.py:172
  33.4 1.4 copy-start
  33.7 0.7 copy-start.2
  34.8 1.0 copy-start.1
  36.6 14.8 %collective-permute-start.9 = (bf16[1,2,1]{2,1,0:T(2,128)(2,1)S(1)}, bf16[1,2,1]{2,1,0:T(2,128)(2,1)S(1)}, u32[]{:S(2)}, u32[]{:S(2)}) collective-permute-start(bf16[1,2,1]{2,1,0:T(2,128)(2,1)S(1)} %get-tuple-element.61), channel_id=1, source_target_pairs={{16,0},{32,16},{48,32},{64,48},{80,64},{96,80},{112,96},{128,112},... | collective-permute-start | bytes 20 | tf_op jit(solution)/shard_map/ppermute | solution.py:27
  39.2 12.3 %collective-permute-start.8 = (bf16[1,2,1]{2,1,0:T(2,128)(2,1)S(1)}, bf16[1,2,1]{2,1,0:T(2,128)(2,1)S(1)}, u32[]{:S(2)}, u32[]{:S(2)}) collective-permute-start(bf16[1,2,1]{2,1,0:T(2,128)(2,1)S(1)} %get-tuple-element.60), channel_id=1, source_target_pairs={{0,16},{16,32},{32,48},{48,64},{64,80},{80,96},{96,112},{112,128},... | collective-permute-start | bytes 20 | tf_op jit(solution)/shard_map/ppermute | solution.py:27
  45.6 6.0 %collective-permute-start.6 = (bf16[1,1,2]{2,1,0:T(2,128)(2,1)S(1)}, bf16[1,1,2]{2,1,0:T(2,128)(2,1)S(1)}, u32[]{:S(2)}, u32[]{:S(2)}) collective-permute-start(bf16[1,1,2]{2,1,0:T(2,128)(2,1)S(1)} %get-tuple-element.54), channel_id=1, source_target_pairs={{0,128},{16,144},{32,160},{48,176},{64,192},{80,208},{96,224},{112... | collective-permute-start | bytes 20 | tf_op jit(solution)/shard_map/ppermute | solution.py:27
  52.1 26.0 %all-to-all-start = ((bf16[16,16,384]{2,0,1:T(8,128)(2,1)}), bf16[16,16,384]{2,0,1:T(8,128)(2,1)S(1)}, u32[]{:S(2)}, u32[]{:S(2)}) async-start(bf16[16,16,384]{2,0,1:T(8,128)(2,1)} %bitcast.223), calls=%async_computation | async-start | bytes 393216 | tf_op jit(solution)/shard_map/all_to_all | solution.py:173
  78.1 19.7 %all-to-all-start.2 = ((bf16[16,16,384]{2,0,1:T(8,128)(2,1)}), bf16[16,16,384]{2,0,1:T(8,128)(2,1)S(1)}, u32[]{:S(2)}, u32[]{:S(2)}) async-start(bf16[16,16,384]{2,0,1:T(8,128)(2,1)} %bitcast.221), calls=%async_computation.2 | async-start | bytes 393216 | tf_op jit(solution)/shard_map/all_to_all | solution.py:171
  82.1 69.3 %collective-permute-start.19 = (bf16[1,1,2,64,3,128]{5,3,4,2,1,0:T(8,128)(2,1)S(1)}, bf16[1,1,2,64,3,128]{5,3,4,2,1,0:T(8,128)(2,1)S(1)}, u32[]{:S(2)}, u32[]{:S(2)}) collective-permute-start(bf16[1,1,2,64,3,128]{5,3,4,2,1,0:T(8,128)(2,1)S(1)} %get-tuple-element.37), channel_id=1, source_target_pairs={{128,0},{144,16},{160,32},{176,48},{192,64},{208,80},{224,96},{240... | collective-permute-start | bytes 294920 | tf_op jit(solution)/shard_map/ppermute | solution.py:27
  83.4 70.0 %collective-permute-start.14 = (bf16[1,2,1,64,3,128]{5,3,4,2,1,0:T(8,128)(2,1)S(1)}, bf16[1,2,1,64,3,128]{5,3,4,2,1,0:T(8,128)(2,1)S(1)}, u32[]{:S(2)}, u32[]{:S(2)}) collective-permute-start(bf16[1,2,1,64,3,128]{5,3,4,2,1,0:T(8,128)(2,1)S(1)} %get-tuple-element.41), channel_id=1, source_target_pairs={{16,0},{32,16},{48,32},{64,48},{80,64},{96,80},{112,96},{128,112},... | collective-permute-start | bytes 294920 | tf_op jit(solution)/shard_map/ppermute | solution.py:27
  85.4 73.9 %collective-permute-start.13 = (bf16[1,2,1,64,3,128]{5,3,4,2,1,0:T(8,128)(2,1)S(1)}, bf16[1,2,1,64,3,128]{5,3,4,2,1,0:T(8,128)(2,1)S(1)}, u32[]{:S(2)}, u32[]{:S(2)}) collective-permute-start(bf16[1,2,1,64,3,128]{5,3,4,2,1,0:T(8,128)(2,1)S(1)} %get-tuple-element.40), channel_id=1, source_target_pairs={{0,16},{16,32},{32,48},{48,64},{64,80},{80,96},{96,112},{112,128},... | collective-permute-start | bytes 294920 | tf_op jit(solution)/shard_map/ppermute | solution.py:27
  92.1 71.2 %collective-permute-start.11 = (bf16[1,1,2,64,3,128]{5,3,4,2,1,0:T(8,128)(2,1)S(1)}, bf16[1,1,2,64,3,128]{5,3,4,2,1,0:T(8,128)(2,1)S(1)}, u32[]{:S(2)}, u32[]{:S(2)}) collective-permute-start(bf16[1,1,2,64,3,128]{5,3,4,2,1,0:T(8,128)(2,1)S(1)} %get-tuple-element.36), channel_id=1, source_target_pairs={{0,128},{16,144},{32,160},{48,176},{64,192},{80,208},{96,224},{112... | collective-permute-start | bytes 294920 | tf_op jit(solution)/shard_map/ppermute | solution.py:27
  95.8 5.4 %collective-permute-start.18 = (bf16[1,1,1,64,3,128]{5,3,4,2,1,0:T(8,128)(2,1)S(1)}, bf16[1,1,1,64,3,128]{5,3,4,2,1,0:T(8,128)(2,1)S(1)}, u32[]{:S(2)}, u32[]{:S(2)}) collective-permute-start(bf16[1,1,1,64,3,128]{5,3,4,2,1,0:T(8,128)(2,1)S(1)} %get-tuple-element.34), channel_id=1, source_target_pairs={{112,0},{128,16},{144,32},{160,48},{176,64},{192,80},{208,96},{224... | collective-permute-start | bytes 147464 | tf_op jit(solution)/shard_map/ppermute | solution.py:27
  101.2 6.6 %collective-permute-start.12 = (bf16[1,1,1,64,3,128]{5,3,4,2,1,0:T(8,128)(2,1)S(1)}, bf16[1,1,1,64,3,128]{5,3,4,2,1,0:T(8,128)(2,1)S(1)}, u32[]{:S(2)}, u32[]{:S(2)}) collective-permute-start(bf16[1,1,1,64,3,128]{5,3,4,2,1,0:T(8,128)(2,1)S(1)} %get-tuple-element.35), channel_id=1, source_target_pairs={{0,112},{16,128},{32,144},{48,160},{64,176},{80,192},{96,208},{112... | collective-permute-start | bytes 147464 | tf_op jit(solution)/shard_map/ppermute | solution.py:27
  107.8 5.9 %collective-permute-start.10 = (bf16[1,1,1,64,3,128]{5,3,4,2,1,0:T(8,128)(2,1)S(1)}, bf16[1,1,1,64,3,128]{5,3,4,2,1,0:T(8,128)(2,1)S(1)}, u32[]{:S(2)}, u32[]{:S(2)}) collective-permute-start(bf16[1,1,1,64,3,128]{5,3,4,2,1,0:T(8,128)(2,1)S(1)} %get-tuple-element.32), channel_id=1, source_target_pairs={{0,144},{16,160},{32,176},{48,192},{64,208},{80,224},{96,240},{112... | collective-permute-start | bytes 147464 | tf_op jit(solution)/shard_map/ppermute | solution.py:27
  113.7 9.6 %collective-permute-start.20 = (bf16[1,1,1,64,3,128]{5,3,4,2,1,0:T(8,128)(2,1)S(1)}, bf16[1,1,1,64,3,128]{5,3,4,2,1,0:T(8,128)(2,1)S(1)}, u32[]{:S(2)}, u32[]{:S(2)}) collective-permute-start(bf16[1,1,1,64,3,128]{5,3,4,2,1,0:T(8,128)(2,1)S(1)} %get-tuple-element.33), channel_id=1, source_target_pairs={{144,0},{160,16},{176,32},{192,48},{208,64},{224,80},{240,96},{256... | collective-permute-start | bytes 147464 | tf_op jit(solution)/shard_map/ppermute | solution.py:27
  123.3 5.4 %collective-permute-start.21 = (bf16[1,1,1,64,3,128]{5,3,4,2,1,0:T(8,128)(2,1)S(1)}, bf16[1,1,1,64,3,128]{5,3,4,2,1,0:T(8,128)(2,1)S(1)}, u32[]{:S(2)}, u32[]{:S(2)}) collective-permute-start(bf16[1,1,1,64,3,128]{5,3,4,2,1,0:T(8,128)(2,1)S(1)} %get-tuple-element.28), channel_id=1, source_target_pairs={{112,0},{128,16},{144,32},{160,48},{176,64},{192,80},{208,96},{224... | collective-permute-start | bytes 147464 | tf_op jit(solution)/shard_map/ppermute | solution.py:27
  128.7 6.6 %collective-permute-start.2 = (bf16[1,1,1,64,3,128]{5,3,4,2,1,0:T(8,128)(2,1)S(1)}, bf16[1,1,1,64,3,128]{5,3,4,2,1,0:T(8,128)(2,1)S(1)}, u32[]{:S(2)}, u32[]{:S(2)}) collective-permute-start(bf16[1,1,1,64,3,128]{5,3,4,2,1,0:T(8,128)(2,1)S(1)} %get-tuple-element.29), channel_id=1, source_target_pairs={{0,112},{16,128},{32,144},{48,160},{64,176},{80,192},{96,208},{112... | collective-permute-start | bytes 147464 | tf_op jit(solution)/shard_map/ppermute | solution.py:27
  135.3 5.2 %collective-permute-start = (bf16[1,1,1,64,3,128]{5,3,4,2,1,0:T(8,128)(2,1)S(1)}, bf16[1,1,1,64,3,128]{5,3,4,2,1,0:T(8,128)(2,1)S(1)}, u32[]{:S(2)}, u32[]{:S(2)}) collective-permute-start(bf16[1,1,1,64,3,128]{5,3,4,2,1,0:T(8,128)(2,1)S(1)} %get-tuple-element.26), channel_id=1, source_target_pairs={{0,144},{16,160},{32,176},{48,192},{64,208},{80,224},{96,240},{112... | collective-permute-start | bytes 147464 | tf_op jit(solution)/shard_map/ppermute | solution.py:27
  140.6 9.6 %collective-permute-start.23 = (bf16[1,1,1,64,3,128]{5,3,4,2,1,0:T(8,128)(2,1)S(1)}, bf16[1,1,1,64,3,128]{5,3,4,2,1,0:T(8,128)(2,1)S(1)}, u32[]{:S(2)}, u32[]{:S(2)}) collective-permute-start(bf16[1,1,1,64,3,128]{5,3,4,2,1,0:T(8,128)(2,1)S(1)} %get-tuple-element.27), channel_id=1, source_target_pairs={{144,0},{160,16},{176,32},{192,48},{208,64},{224,80},{240,96},{256... | collective-permute-start | bytes 147464 | tf_op jit(solution)/shard_map/ppermute | solution.py:27
  150.2 15.4 %collective-permute-start.22 = (bf16[1,1,2,64,3,128]{5,3,4,2,1,0:T(8,128)(2,1)S(1)}, bf16[1,1,2,64,3,128]{5,3,4,2,1,0:T(8,128)(2,1)S(1)}, u32[]{:S(2)}, u32[]{:S(2)}) collective-permute-start(bf16[1,1,2,64,3,128]{5,3,4,2,1,0:T(8,128)(2,1)S(1)} %get-tuple-element.31), channel_id=1, source_target_pairs={{128,0},{144,16},{160,32},{176,48},{192,64},{208,80},{224,96},{240... | collective-permute-start | bytes 294920 | tf_op jit(solution)/shard_map/ppermute | solution.py:27
  151.5 14.1 %collective-permute-start.4 = (bf16[1,2,1,64,3,128]{5,3,4,2,1,0:T(8,128)(2,1)S(1)}, bf16[1,2,1,64,3,128]{5,3,4,2,1,0:T(8,128)(2,1)S(1)}, u32[]{:S(2)}, u32[]{:S(2)}) collective-permute-start(bf16[1,2,1,64,3,128]{5,3,4,2,1,0:T(8,128)(2,1)S(1)} %get-tuple-element.39), channel_id=1, source_target_pairs={{16,0},{32,16},{48,32},{64,48},{80,64},{96,80},{112,96},{128,112},... | collective-permute-start | bytes 294920 | tf_op jit(solution)/shard_map/ppermute | solution.py:27
  153.4 12.2 %collective-permute-start.3 = (bf16[1,2,1,64,3,128]{5,3,4,2,1,0:T(8,128)(2,1)S(1)}, bf16[1,2,1,64,3,128]{5,3,4,2,1,0:T(8,128)(2,1)S(1)}, u32[]{:S(2)}, u32[]{:S(2)}) collective-permute-start(bf16[1,2,1,64,3,128]{5,3,4,2,1,0:T(8,128)(2,1)S(1)} %get-tuple-element.38), channel_id=1, source_target_pairs={{0,16},{16,32},{32,48},{48,64},{64,80},{80,96},{96,112},{112,128},... | collective-permute-start | bytes 294920 | tf_op jit(solution)/shard_map/ppermute | solution.py:27
  159.2 6.8 %collective-permute-start.1 = (bf16[1,1,2,64,3,128]{5,3,4,2,1,0:T(8,128)(2,1)S(1)}, bf16[1,1,2,64,3,128]{5,3,4,2,1,0:T(8,128)(2,1)S(1)}, u32[]{:S(2)}, u32[]{:S(2)}) collective-permute-start(bf16[1,1,2,64,3,128]{5,3,4,2,1,0:T(8,128)(2,1)S(1)} %get-tuple-element.30), channel_id=1, source_target_pairs={{0,128},{16,144},{32,160},{48,176},{64,192},{80,208},{96,224},{112... | collective-permute-start | bytes 294920 | tf_op jit(solution)/shard_map/ppermute | solution.py:27
where the time goes:
time: 199 us; the launch traced here: 198 us
  starting transfers between devices  104 us (52%)
  waiting for transfers between devices  48.6 us (24%)
  blocking collectives  26.6 us (13%)
  local copies, waits for them, and re-layouts  6.35 us (3%)
  matrix products  5.75 us (3%)
  other arithmetic  3.89 us (2%)
  between operations  3.25 us (2%)
    ppermute x24, starting transfers between devices, shifted(): return lax.ppermute(shard, axis, pairs)  73.1 us
    ppermute x24, waiting for transfers between devices, shifted(): return lax.ppermute(shard, axis, pairs)  34.7 us
    all_to_all x1, blocking collectives, on_device(): lax.all_to_all(result.reshape(patch_tokens, head_count * HDIM), 'uly', sp...  26.6 us
    all_to_all x1, starting transfers between devices, on_device(): lax.all_to_all(keys, 'uly', split_axis=1, concat_axis=0, tiled=True)  14.9 us
    all_to_all x1, waiting for transfers between devices, on_device(): lax.all_to_all(values, 'uly', split_axis=1, concat_axis=0, tiled=True)  13.9 us
    all_to_all x1, starting transfers between devices, on_device(): lax.all_to_all(values, 'uly', split_axis=1, concat_axis=0, tiled=True)  11.7 us
  transfers between devices with their start and end apart: 27, of which 9 were waited for; matrix products, arithmetic and copies ran while one was open for 4% of the time, Pallas kernels for 0%

commit v1 on v0

v1 whole, which is shorter than its diff:
```python
import functools
import math

import jax
import jax.numpy as jnp
from jax import lax
from jax.experimental import pallas as pl
from jax.experimental.pallas import tpu as pltpu
from jax.sharding import PartitionSpec as P

HDIM = 128
TILE = 64
ROWB, COLB = 4, 8
ULY = 16
PART = 16
LOCAL_HEADS = 3
NEG = -1e30
EXP_SCALE = math.log2(math.e) / math.sqrt(HDIM)
MOVES = [(a, b) for a in (-1, 0, 1) for b in (-1, 0, 1)]


def near(move):
    return pl.ds(1, 2) if move == 0 else pl.ds(2, 1) if move == 1 else pl.ds(1, 1)


def far(move):
    return pl.ds(1, 2) if move == 0 else pl.ds(0, 1) if move == 1 else pl.ds(3, 1)


def wait_bytes(ref, sem):
    pltpu.make_async_copy(ref, ref, sem).wait()


def kernel(count_s, mask_s, q_in, k_in, v_in, out, kv, qb, ob, cnt, bias,
           own_sem, send_sem, halo_send, cnt_send, out_send, out_own,
           in_recv, halo_recv, cnt_recv, out_recv):
    blk = lax.axis_index("blk")
    z = lax.axis_index("uly")
    row, col = blk // COLB, blk % COLB

    def neighbour(a, b):
        return lax.rem(row + a + ROWB, ROWB) * COLB + lax.rem(col + b + COLB, COLB)

    others = [m for m in MOVES if m != (0, 0)]
    barrier = pltpu.get_barrier_semaphore()

    def greet(d, carry):
        pl.semaphore_signal(barrier, inc=1, device_id=(blk, lax.rem(z + d, ULY)),
                            device_id_type=pl.DeviceIdType.MESH)
        return carry

    lax.fori_loop(1, ULY, greet, 0)
    for a, b in others:
        pl.semaphore_signal(barrier, inc=1, device_id=(neighbour(a, b), z),
                            device_id_type=pl.DeviceIdType.MESH)

    def columns(peer, head):
        return pl.ds(pl.multiple_of((peer * LOCAL_HEADS + head) * HDIM, HDIM), HDIM)

    def slot(array, head, part):
        rows = pl.ds(pl.multiple_of(lax.rem(part, 4) * PART, PART), PART)
        if array == 2:
            return qb.at[head, pl.ds(pl.multiple_of(part * PART, PART), PART)]
        return kv.at[head, array, 1 + part // 8, 1 + lax.rem(part // 4, 2), rows]

    sources = (k_in, v_in, q_in)

    own = []
    for head in range(LOCAL_HEADS):
        for array in range(3):
            copy = pltpu.make_async_copy(sources[array].at[:, columns(z, head)],
                                         slot(array, head, z), own_sem.at[head, array])
            copy.start()
            own.append(copy)

    for tile in range(4):
        cnt[4, tile:tile + 1, :] = jnp.full((1, 128), count_s[tile], jnp.int32)
    for tile in range(4):
        cnt[4, tile + 4:tile + 5, :] = jnp.zeros((1, 128), jnp.int32)

    pl.semaphore_wait(barrier, ULY - 1 + len(others))

    def ring(step):
        return 8 + (step + 1) // 2 * (2 * lax.rem(step, 2) - 1)

    def scatter(array, head):
        def body(step, carry):
            peer = lax.rem(z + ring(step), ULY)
            pltpu.make_async_remote_copy(
                src_ref=sources[array].at[:, columns(peer, head)],
                dst_ref=slot(array, head, z),
                send_sem=send_sem.at[array],
                recv_sem=in_recv.at[head, array],
                device_id=(blk, peer),
                device_id_type=pl.DeviceIdType.MESH,
            ).start()
            return carry

        lax.fori_loop(0, ULY - 1, body, 0)

    def arrived(array, head):
        own[head * 3 + array].wait()
        wait_bytes(qb.at[head, pl.ds(0, (ULY - 1) * PART)], in_recv.at[head, array])

    def halo(array, head):
        for a, b in others:
            pltpu.make_async_remote_copy(
                src_ref=kv.at[head, array, near(a), near(b)],
                dst_ref=kv.at[head, array, far(a), far(b)],
                send_sem=halo_send,
                recv_sem=halo_recv.at[head, array],
                device_id=(neighbour(a, b), z),
                device_id_type=pl.DeviceIdType.MESH,
            ).start()

    def halo_arrived(array, head):
        wait_bytes(kv.at[head, array, pl.ds(0, 3)], halo_recv.at[head, array])

    scatter(0, 0)
    scatter(1, 0)
    for index, (a, b) in enumerate(MOVES):
        if (a, b) != (0, 0):
            pltpu.make_async_remote_copy(
                src_ref=cnt.at[4],
                dst_ref=cnt.at[8 - index],
                send_sem=cnt_send,
                recv_sem=cnt_recv,
                device_id=(neighbour(a, b), z),
                device_id_type=pl.DeviceIdType.MESH,
            ).start()
    scatter(2, 0)
    scatter(0, 1)
    scatter(1, 1)

    def build_bias():
        wait_bytes(cnt.at[pl.ds(0, 8)], cnt_recv)
        lane = lax.broadcasted_iota(jnp.int32, (1, 128), 1)
        low = lane < TILE
        place = lax.rem(lane, TILE)

        def tile_count(r, c):
            a, b = (r + 1) // 2 - 1, (c + 1) // 2 - 1
            tile = (r + 1) % 2 * 2 + (c + 1) % 2
            return cnt[(a + 1) * 3 + b + 1, tile:tile + 1, :]

        for r in range(4):
            for half in range(2):
                live = place < jnp.where(low, tile_count(r, 2 * half), tile_count(r, 2 * half + 1))
                for tile in range(4):
                    qr, qc = tile // 2, tile % 2
                    kr = r - qr
                    if not 0 <= kr < 3:
                        continue
                    picks = []
                    for c in (2 * half, 2 * half + 1):
                        e = c - qc
                        picks.append(mask_s[tile, 9 + 3 * kr + e] if 0 <= e < 3 else 0)
                    picked = jnp.where(low, picks[0], picks[1])
                    start = kr * 256 + half * 128
                    bias[tile:tile + 1, start:start + 128] = jnp.where(
                        live & (picked > 0), 0.0, NEG).astype(jnp.float32)

    def compute(head):
        for qr in range(2):
            q = qb[head, qr * 128:(qr + 1) * 128, :]
            k = kv[head, 0, qr:qr + 3].reshape(768, HDIM)
            v = kv[head, 1, qr:qr + 3].reshape(768, HDIM)
            raw = lax.dot_general(q, k, (((1,), (1,)), ((), ())),
                                  preferred_element_type=jnp.float32)
            raw = (raw.reshape(2, TILE, 768) + bias[2 * qr:2 * qr + 2, :].reshape(2, 1, 768)).reshape(128, 768)
            peak = jnp.max(raw, axis=1, keepdims=True)
            expo = jnp.exp2((raw - peak) * EXP_SCALE)
            total = jnp.sum(expo, axis=1, keepdims=True)
            summed = jnp.dot(expo.astype(jnp.bfloat16), v, preferred_element_type=jnp.float32)
            ob[head, qr * 128:(qr + 1) * 128, :] = (summed / total).astype(jnp.bfloat16)

    def gather(head):
        def body(step, carry):
            peer = lax.rem(z + ring(step), ULY)
            pltpu.make_async_remote_copy(
                src_ref=ob.at[head, pl.ds(pl.multiple_of(peer * PART, PART), PART)],
                dst_ref=out.at[:, columns(z, head)],
                send_sem=out_send,
                recv_sem=out_recv,
                device_id=(blk, peer),
                device_id_type=pl.DeviceIdType.MESH,
            ).start()
            return carry

        lax.fori_loop(0, ULY - 1, body, 0)
        copy = pltpu.make_async_copy(
            ob.at[head, pl.ds(pl.multiple_of(z * PART, PART), PART)],
            out.at[:, columns(z, head)], out_own.at[head])
        copy.start()
        return copy

    last = []
    for head in range(LOCAL_HEADS):
        arrived(0, head)
        halo(0, head)
        arrived(1, head)
        halo(1, head)
        if head + 1 < LOCAL_HEADS:
            scatter(2, head + 1)
        if head == 0:
            scatter(0, 2)
            scatter(1, 2)
            build_bias()
        arrived(2, head)
        halo_arrived(0, head)
        halo_arrived(1, head)
        compute(head)
        last.append(gather(head))

    sent = pl.ds(0, LOCAL_HEADS * (ULY - 1) * HDIM)
    for array in range(3):
        wait_bytes(sources[array].at[:, sent], send_sem.at[array])
    for head in range(LOCAL_HEADS):
        for array in range(2):
            wait_bytes(kv.at[head, array, pl.ds(0, 3)], halo_send)
    wait_bytes(cnt.at[pl.ds(0, 8)], cnt_send)
    for copy in last:
        copy.wait()
    wait_bytes(out.at[:, sent], out_send)
    wait_bytes(out.at[:, sent], out_recv)


def on_device(queries, keys, values, window_mask, valid_count):
    heads = LOCAL_HEADS
    dma = pltpu.SemaphoreType.DMA
    return pl.pallas_call(
        kernel,
        out_shape=jax.ShapeDtypeStruct(queries.shape, queries.dtype),
        in_specs=[pl.BlockSpec(memory_space=pltpu.SMEM)] * 2 + [pl.BlockSpec(memory_space=pl.ANY)] * 3,
        out_specs=pl.BlockSpec(memory_space=pl.ANY),
        scratch_shapes=[
            pltpu.VMEM((heads, 2, 4, 4, TILE, HDIM), jnp.bfloat16),
            pltpu.VMEM((heads, 256, HDIM), jnp.bfloat16),
            pltpu.VMEM((heads, 256, HDIM), jnp.bfloat16),
            pltpu.VMEM((9, 8, 128), jnp.int32),
            pltpu.VMEM((8, 768), jnp.float32),
            dma((heads, 3)), dma((3,)), dma, dma, dma, dma((heads,)),
            dma((heads, 3)), dma((heads, 2)), dma, dma,
        ],
        compiler_params=pltpu.CompilerParams(
            collective_id=0, has_side_effects=True, vmem_limit_bytes=24 * 1024 * 1024),
    )(valid_count, window_mask, queries, keys, values)


def solution(mesh):
    in_specs = (
        P(("blk", "uly"), None),
        P(("blk", "uly"), None),
        P(("blk", "uly"), None),
        P("blk", None),
        P("blk"),
    )
    out_specs = P(("blk", "uly"), None)
    return jax.shard_map(
        on_device, mesh=mesh, in_specs=in_specs, out_specs=out_specs, check_vma=False
    )
```

time: 199 us -> 62.2 us (0.31)
  the two profiles are of different devices: /device:TPU:25 before, /device:TPU:8 now
where the time goes in v1:
time: 62.2 us; the launch traced here: 62 us
  Pallas kernels  57.2 us (92%)
  local copies, waits for them, and re-layouts  4.79 us (8%)
    pallas_call x1, Pallas kernels, on_device(): pl.pallas_call(kernel, out_shape=jax.ShapeDtypeStruct(queries.shape, quer...  57.2 us
    unnamed x11, local copies, waits for them, and re-layouts  4.79 us

profile of v1, /device:TPU:8, one launch (start us, length us, event | category | flops | bytes accessed | tf_op | source)
XLA Modules:
  0.0 62.0 jit_solution(12312515174731840225)
XLA Ops:
  0.0 0.0 copy-start
  0.0 0.9 %copy-done = bf16[16,6144]{1,0:T(8,128)(2,1)S(1)} copy-done((bf16[16,6144]{1,0:T(8,128)(2,1)S(1)}, bf16[16,6144]{1,0:T(8,128)(2,1)}, u32[]{:S(2)}) %copy-start) | copy-done | bytes 196632
  0.9 0.0 copy-start.1
  0.9 0.9 %copy-done.1 = bf16[16,6144]{1,0:T(8,128)(2,1)S(1)} copy-done((bf16[16,6144]{1,0:T(8,128)(2,1)S(1)}, bf16[16,6144]{1,0:T(8,128)(2,1)}, u32[]{:S(2)}) %copy-start.1) | copy-done | bytes 196632
  1.9 0.0 copy-start.2
  1.9 0.9 %copy-done.2 = bf16[16,6144]{1,0:T(8,128)(2,1)S(1)} copy-done((bf16[16,6144]{1,0:T(8,128)(2,1)S(1)}, bf16[16,6144]{1,0:T(8,128)(2,1)}, u32[]{:S(2)}) %copy-start.2) | copy-done | bytes 196632
  2.8 0.0 copy-start.3
  2.8 0.7 %copy-done.3 = s32[4,27]{1,0:T(4,128)S(1)} copy-done((s32[4,27]{1,0:T(4,128)S(1)}, s32[4,27]{1,0:T(4,128)}, u32[]{:S(2)}) %copy-start.3) | copy-done | bytes 456
  3.5 0.0 copy-start.4
  3.5 0.7 %copy-done.4 = s32[4]{0:T(128)S(1)} copy-done((s32[4]{0:T(128)S(1)}, s32[4]{0:T(128)}, u32[]{:S(2)}) %copy-start.4) | copy-done | bytes 40
  4.1 57.2 %shard_map.55 = bf16[16,6144]{1,0:T(8,128)(2,1)S(1)} custom-call(s32[4]{0:T(128)S(1)} %copy-done.4, s32[4,27]{1,0:T(4,128)S(1)} %copy-done.3, bf16[16,6144]{1,0:T(8,128)(2,1)S(1)} %copy-done, bf16[16,6144]{1,0:T(8,128)(2,1)S(1)} %copy-done.1, bf16[16,6144]{1,0:T(8,128)(2,1)S(1)} %copy-done.2), custom_call_target="tpu_custom_call" | custom-call | tf_op jit(solution)/shard_map/pallas_call | solution.py:231
  61.3 0.7 %copy.7 = bf16[16,6144]{1,0:T(8,128)(2,1)} copy(bf16[16,6144]{1,0:T(8,128)(2,1)S(1)} %shard_map.55) | data formatting | bytes 393216
Async XLA Ops:
  0.0 0.9 %copy-start = (bf16[16,6144]{1,0:T(8,128)(2,1)S(1)}, bf16[16,6144]{1,0:T(8,128)(2,1)}, u32[]{:S(2)}) copy-start(bf16[16,6144]{1,0:T(8,128)(2,1)} %q_in.1) | copy-start | bytes 589828
  0.9 0.9 %copy-start.1 = (bf16[16,6144]{1,0:T(8,128)(2,1)S(1)}, bf16[16,6144]{1,0:T(8,128)(2,1)}, u32[]{:S(2)}) copy-start(bf16[16,6144]{1,0:T(8,128)(2,1)} %k_in.1) | copy-start | bytes 589828
  1.9 0.9 %copy-start.2 = (bf16[16,6144]{1,0:T(8,128)(2,1)S(1)}, bf16[16,6144]{1,0:T(8,128)(2,1)}, u32[]{:S(2)}) copy-start(bf16[16,6144]{1,0:T(8,128)(2,1)} %v_in.1) | copy-start | bytes 589828
  2.8 0.7 %copy-start.3 = (s32[4,27]{1,0:T(4,128)S(1)}, s32[4,27]{1,0:T(4,128)}, u32[]{:S(2)}) copy-start(s32[4,27]{1,0:T(4,128)} %mask_s.1) | copy-start | bytes 1300
  3.5 0.7 %copy-start.4 = (s32[4]{0:T(128)S(1)}, s32[4]{0:T(128)}, u32[]{:S(2)}) copy-start(s32[4]{0:T(128)} %count_s.1) | copy-start | bytes 52

commit v2 on v1

v2 whole, which is shorter than its diff:
```python
import math

import jax
import jax.numpy as jnp
from jax import lax
from jax.experimental import pallas as pl
from jax.experimental.pallas import tpu as pltpu
from jax.sharding import PartitionSpec as P

HDIM = 128
TILE = 64
ROWB, COLB = 4, 8
ULY = 16
HALF = ULY // 2
PART = 16
LOCAL_HEADS = 3
NEG = -1e30
EXP_SCALE = math.log2(math.e) / math.sqrt(HDIM)
MOVES = [(a, b) for a in (-1, 0, 1) for b in (-1, 0, 1)]
MESH = pl.DeviceIdType.MESH

ALL, FAR, NEAR = (0, ULY - 1), (0, 7), (7, ULY - 1)
SCHEDULE = (
    ('k', 0, ALL),
    ('v', 0, ALL),
    ('counts', 0),
    ('q', 0, ALL),
    ('k', 1, ALL),
    ('v', 1, ALL),
    ('k', 2, ALL),
    ('v', 2, ALL),
    ('q', 1, FAR),
    ('q', 2, FAR),
    ('q', 1, NEAR),
    ('q', 2, NEAR),
    ('hk', 0),
    ('hv', 0),
    ('bias', 0),
    ('hk', 1),
    ('hv', 1),
    ('c', 0, 0),
    ('c', 0, 1),
    ('o', 0, ALL, 2),
    ('hk', 2),
    ('hv', 2),
    ('c', 1, 0),
    ('o', 1, FAR, 0),
    ('c', 1, 1),
    ('o', 1, FAR, 1),
    ('c', 2, 0),
    ('o', 2, FAR, 0),
    ('c', 2, 1),
    ('o', 2, FAR, 1),
    ('o', 1, NEAR, 2),
    ('o', 2, NEAR, 2),
)


def near(move):
    return pl.ds(1, 2) if move == 0 else pl.ds(2, 1) if move == 1 else pl.ds(1, 1)


def far(move):
    return pl.ds(1, 2) if move == 0 else pl.ds(0, 1) if move == 1 else pl.ds(3, 1)


def wait_bytes(ref, sem):
    pltpu.make_async_copy(ref, ref, sem).wait()


def kernel(count_in, mask_in, q_in, k_in, v_in, out, kv, qb, ob, cnt, bias, count_s, mask_s,
           small, send_sem, halo_send, cnt_send, out_send,
           kv_recv, q_recv, halo_recv, cnt_recv, out_recv):
    blk = lax.axis_index("blk")
    z = lax.axis_index("uly")
    half = z // HALF
    row, col = blk // COLB, blk % COLB

    up, down = row > 0, row < ROWB - 1
    left, right = col > 0, col < COLB - 1
    others = sorted((m for m in MOVES if m != (0, 0)), key=lambda m: -abs(m[0]) - abs(m[1]))
    barrier = pltpu.get_barrier_semaphore()
    cnt[...] = jnp.zeros_like(cnt)

    def to_neighbour(a, b):
        return (blk + a * COLB + b, z)

    def if_inside(a, b):
        inside = [have for have, wanted in ((up, a < 0), (down, a > 0), (left, b < 0), (right, b > 0)) if wanted]
        return pl.when(inside[0] if len(inside) == 1 else inside[0] & inside[1])

    def ring(step):
        return 8 + (step + 1) // 2 * (2 * lax.rem(step, 2) - 1)

    def greet(d, carry):
        pl.semaphore_signal(barrier, inc=1, device_id=(blk, lax.rem(z + ring(d), ULY)), device_id_type=MESH)
        return carry

    lax.fori_loop(0, ULY - 1, greet, 0)
    for a, b in others:
        @if_inside(a, b)
        def _():
            pl.semaphore_signal(barrier, inc=1, device_id=to_neighbour(a, b), device_id_type=MESH)

    def columns(peer, head):
        return pl.ds(pl.multiple_of((peer * LOCAL_HEADS + head) * HDIM, HDIM), HDIM)

    def rows_of(part):
        return pl.ds(pl.multiple_of(part * PART, PART), PART)

    def kv_slot(array, head, part):
        return kv.at[head, array, 1 + part // HALF, 1 + lax.rem(part // 4, 2), rows_of(lax.rem(part, 4))]

    kv_in = (k_in, v_in)

    loads = [pltpu.make_async_copy(count_in, count_s, small.at[0]),
             pltpu.make_async_copy(mask_in, mask_s, small.at[1])]
    for copy in loads:
        copy.start()
    for head in range(LOCAL_HEADS):
        for array in range(2):
            pltpu.make_async_copy(kv_in[array].at[:, columns(z, head)], kv_slot(array, head, z),
                                  kv_recv.at[head, array]).start()
        pltpu.make_async_copy(q_in.at[:, columns(z, head)], qb.at[head, rows_of(z)],
                              q_recv.at[head]).start()

    for edge, at in ((~up, 0), (~down, 3)):
        @pl.when(edge)
        def _():
            kv[:, :, at:at + 1] = jnp.zeros((LOCAL_HEADS, 2, 1, 4, TILE, HDIM), kv.dtype)
    for edge, at in ((~left, 0), (~right, 3)):
        @pl.when(edge)
        def _():
            kv[:, :, :, at:at + 1] = jnp.zeros((LOCAL_HEADS, 2, 4, 1, TILE, HDIM), kv.dtype)

    across = 1 + left.astype(jnp.int32) + right.astype(jnp.int32)
    along = 1 + up.astype(jnp.int32) + down.astype(jnp.int32)
    pl.semaphore_wait(barrier, ULY - 2 + across * along)

    def scatter(array, head, steps):
        def body(step, carry):
            peer = lax.rem(z + ring(step), ULY)
            pltpu.make_async_remote_copy(
                src_ref=kv_in[array].at[:, columns(peer, head)],
                dst_ref=kv_slot(array, head, z),
                send_sem=send_sem.at[array],
                recv_sem=kv_recv.at[head, array],
                device_id=(blk, peer),
                device_id_type=MESH,
            ).start()
            return carry

        lax.fori_loop(*steps, body, 0)

    def scatter_queries(head, steps):
        def body(step, carry):
            peer = lax.rem(z + ring(step), ULY)
            pltpu.make_async_remote_copy(
                src_ref=q_in.at[:, columns(peer, head)],
                dst_ref=qb.at[head, rows_of(z)],
                send_sem=send_sem.at[2],
                recv_sem=q_recv.at[head],
                device_id=(blk, peer),
                device_id_type=MESH,
            ).start()
            return carry

        lax.fori_loop(*steps, body, 0)

    def send_counts():
        for copy in loads:
            copy.wait()
        for tile in range(8):
            cnt[4, tile:tile + 1, :] = jnp.full((1, 128), count_s[tile % 4], jnp.int32)
        for a, b in others:
            @if_inside(a, b)
            def _():
                index = (a + 1) * 3 + b + 1
                pltpu.make_async_remote_copy(
                    src_ref=cnt.at[4],
                    dst_ref=cnt.at[8 - index],
                    send_sem=cnt_send.at[index],
                    recv_sem=cnt_recv.at[index],
                    device_id=to_neighbour(a, b),
                    device_id_type=MESH,
                ).start()

    def halo(array, head):
        wait_bytes(qb.at[head], kv_recv.at[head, array])
        for a, b in others:
            @if_inside(a, b)
            def _():
                index = (a + 1) * 3 + b + 1
                pltpu.make_async_remote_copy(
                    src_ref=kv.at[head, array, near(a), near(b)],
                    dst_ref=kv.at[head, array, far(a), far(b)],
                    send_sem=halo_send.at[index],
                    recv_sem=halo_recv.at[head, array, index],
                    device_id=to_neighbour(a, b),
                    device_id_type=MESH,
                ).start()

    def halo_arrived(array, head):
        for a, b in others:
            @if_inside(a, b)
            def _():
                wait_bytes(kv.at[head, array, far(-a), far(-b)],
                           halo_recv.at[head, array, (1 - a) * 3 + 1 - b])

    def build_bias():
        for a, b in others:
            @if_inside(a, b)
            def _():
                wait_bytes(cnt.at[0], cnt_recv.at[(1 - a) * 3 + 1 - b])
        lane = lax.broadcasted_iota(jnp.int32, (1, 128), 1)
        low = lane < TILE
        place = lax.rem(lane, TILE)

        def tile_count(r, c):
            a, b = (r + 1) // 2 - 1, (c + 1) // 2 - 1
            tile = (r + 1) % 2 * 2 + (c + 1) % 2
            return cnt[(a + 1) * 3 + b + 1, tile:tile + 1, :]

        for r in range(4):
            for pair in range(2):
                live = place < jnp.where(low, tile_count(r, 2 * pair), tile_count(r, 2 * pair + 1))
                for tile in range(4):
                    qr, qc = tile // 2, tile % 2
                    kr = r - qr
                    if not 0 <= kr < 3:
                        continue
                    picks = []
                    for c in (2 * pair, 2 * pair + 1):
                        e = c - qc
                        picks.append(mask_s[tile, 9 + 3 * kr + e] if 0 <= e < 3 else 0)
                    picked = jnp.where(low, picks[0], picks[1])
                    start = kr * 256 + pair * 128
                    bias[qr, qc:qc + 1, start:start + 128] = jnp.where(
                        live & (picked > 0), 0.0, NEG).astype(jnp.float32)

    def compute(head, qr):
        rows = pl.ds(pl.multiple_of(qr * 128, 128), 128)
        k = kv[head, 0, pl.ds(qr, 3)].reshape(768, HDIM)
        v = kv[head, 1, pl.ds(qr, 3)].reshape(768, HDIM)
        raw = lax.dot_general(qb[head, rows, :], k, (((1,), (1,)), ((), ())),
                              preferred_element_type=jnp.float32)
        raw = (raw.reshape(2, TILE, 768) + bias[qr].reshape(2, 1, 768)).reshape(128, 768)
        peak = jnp.max(raw, axis=1, keepdims=True)
        expo = jnp.exp2((raw - peak) * EXP_SCALE)
        total = jnp.sum(expo, axis=1, keepdims=True)
        summed = jnp.dot(expo.astype(jnp.bfloat16), v, preferred_element_type=jnp.float32)
        ob[head, rows, :] = (summed / total).astype(jnp.bfloat16)

    def give_back(head, steps, which):
        def body(step, carry):
            peer = lax.rem(z + ring(step), ULY)

            def send():
                pltpu.make_async_remote_copy(
                    src_ref=ob.at[head, rows_of(peer)],
                    dst_ref=out.at[:, columns(z, head)],
                    send_sem=out_send,
                    recv_sem=out_recv,
                    device_id=(blk, peer),
                    device_id_type=MESH,
                ).start()

            if which == 2:
                send()
            else:
                pl.when((peer // HALF == half) == (which == 1))(send)
            return carry

        lax.fori_loop(*steps, body, 0)

    complete = set()
    for step in SCHEDULE:
        op, head, *rest = step
        if op in ("k", "v"):
            scatter("kv".index(op), head, *rest)
        elif op == "q":
            scatter_queries(head, *rest)
        elif op in ("hk", "hv"):
            halo("kv".index(op[1]), head)
        elif op == "counts":
            send_counts()
        elif op == "bias":
            build_bias()
        elif op == "c":
            if head not in complete:
                complete.add(head)
                halo_arrived(0, head)
                halo_arrived(1, head)
                wait_bytes(qb.at[head], q_recv.at[head])
            if rest[0] == 0:
                compute(head, 1 - half)
            else:
                compute(head, half)
                pltpu.make_async_copy(ob.at[head, rows_of(z)], out.at[:, columns(z, head)], out_recv).start()
        elif op == "o":
            give_back(head, *rest)

    sent = pl.ds(0, LOCAL_HEADS * (ULY - 1) * HDIM)
    for array in range(2):
        wait_bytes(kv_in[array].at[:, sent], send_sem.at[array])
    wait_bytes(q_in.at[:, sent], send_sem.at[2])
    for a, b in others:
        @if_inside(a, b)
        def _():
            index = (a + 1) * 3 + b + 1
            wait_bytes(kv.at[:, :, near(a), near(b)], halo_send.at[index])
            wait_bytes(cnt.at[4], cnt_send.at[index])
    wait_bytes(out.at[:, sent], out_send)
    wait_bytes(out, out_recv)


def on_device(queries, keys, values, window_mask, valid_count):
    heads = LOCAL_HEADS
    dma = pltpu.SemaphoreType.DMA
    return pl.pallas_call(
        kernel,
        out_shape=jax.ShapeDtypeStruct(queries.shape, queries.dtype),
        in_specs=[pl.BlockSpec(memory_space=pl.ANY)] * 5,
        out_specs=pl.BlockSpec(memory_space=pltpu.VMEM),
        scratch_shapes=[
            pltpu.VMEM((heads, 2, 4, 4, TILE, HDIM), jnp.bfloat16),
            pltpu.VMEM((heads, 256, HDIM), jnp.bfloat16),
            pltpu.VMEM((heads, 256, HDIM), jnp.bfloat16),
            pltpu.VMEM((9, 8, 128), jnp.int32),
            pltpu.VMEM((2, 2, 768), jnp.float32),
            pltpu.SMEM((4,), jnp.int32),
            pltpu.SMEM((4, 27), jnp.int32),
            dma((2,)), dma((3,)), dma((9,)), dma((9,)), dma,
            dma((heads, 2)), dma((heads,)), dma((heads, 2, 9)), dma((9,)), dma,
        ],
        compiler_params=pltpu.CompilerParams(
            collective_id=0, has_side_effects=True, vmem_limit_bytes=56 * 1024 * 1024),
    )(valid_count, window_mask, queries, keys, values)


def solution(mesh):
    in_specs = (
        P(("blk", "uly"), None),
        P(("blk", "uly"), None),
        P(("blk", "uly"), None),
        P("blk", None),
        P("blk"),
    )
    out_specs = P(("blk", "uly"), None)
    return jax.shard_map(
        on_device, mesh=mesh, in_specs=in_specs, out_specs=out_specs, check_vma=False
    )
```

time: 62.2 us -> 55.8 us (0.90)
  the two profiles are of different devices: /device:TPU:8 before, /device:TPU:2 now
where the time goes in v2:
time: 55.8 us; the launch traced here: 55.6 us
  Pallas kernels  54 us (97%)
  local copies, waits for them, and re-layouts  1.62 us (3%)
    pallas_call x1, Pallas kernels, on_device(): pl.pallas_call(kernel, out_shape=jax.ShapeDtypeStruct(queries.shape, quer...  54 us
    unnamed x1, local copies, waits for them, and re-layouts  1.62 us

profile of v2, /device:TPU:2, one launch (start us, length us, event | category | flops | bytes accessed | tf_op | source)
XLA Modules:
  0.0 55.6 jit_solution(10085195246270939015)
XLA Ops:
  0.0 54.0 %shard_map.55 = bf16[16,6144]{1,0:T(8,128)(2,1)} custom-call(s32[4]{0:T(128)} %count_in.1, s32[4,27]{1,0:T(4,128)} %mask_in.1, bf16[16,6144]{1,0:T(8,128)(2,1)} %q_in.1, bf16[16,6144]{1,0:T(8,128)(2,1)} %k_in.1, bf16[16,6144]{1,0:T(8,128)(2,1)} %v_in.1), custom_call_target="tpu_custom_call" | custom-call | tf_op jit(solution)/shard_map/pallas_call | solution.py:320
  54.0 1.6 %copy.7 = bf16[16,6144]{1,0:T(8,128)(2,1)} copy(bf16[16,6144]{1,0:T(8,128)(2,1)} %shard_map.55) | data formatting | bytes 393216

commit v3 on v2

--- a/solution.py
+++ b/solution.py
@@ -20,42 +20,6 @@
 MESH = pl.DeviceIdType.MESH
 
 ALL, FAR, NEAR = (0, ULY - 1), (0, 7), (7, ULY - 1)
-SCHEDULE = (
-    ('k', 0, ALL),
-    ('v', 0, ALL),
-    ('counts', 0),
-    ('q', 0, ALL),
-    ('k', 1, ALL),
-    ('v', 1, ALL),
-    ('k', 2, ALL),
-    ('v', 2, ALL),
-    ('q', 1, FAR),
-    ('q', 2, FAR),
-    ('q', 1, NEAR),
-    ('q', 2, NEAR),
-    ('hk', 0),
-    ('hv', 0),
-    ('bias', 0),
-    ('hk', 1),
-    ('hv', 1),
-    ('c', 0, 0),
-    ('c', 0, 1),
-    ('o', 0, ALL, 2),
-    ('hk', 2),
-    ('hv', 2),
-    ('c', 1, 0),
-    ('o', 1, FAR, 0),
-    ('c', 1, 1),
-    ('o', 1, FAR, 1),
-    ('c', 2, 0),
-    ('o', 2, FAR, 0),
-    ('c', 2, 1),
-    ('o', 2, FAR, 1),
-    ('o', 1, NEAR, 2),
-    ('o', 2, NEAR, 2),
-)
-
-
 def near(move):
     return pl.ds(1, 2) if move == 0 else pl.ds(2, 1) if move == 1 else pl.ds(1, 1)
 
@@ -70,7 +34,7 @@
 
 def kernel(count_in, mask_in, q_in, k_in, v_in, out, kv, qb, ob, cnt, bias, count_s, mask_s,
            small, send_sem, halo_send, cnt_send, out_send,
-           kv_recv, q_recv, halo_recv, cnt_recv, out_recv):
+           in_recv, halo_recv, cnt_recv, out_recv):
     blk = lax.axis_index("blk")
     z = lax.axis_index("uly")
     half = z // HALF
@@ -108,21 +72,21 @@
     def rows_of(part):
         return pl.ds(pl.multiple_of(part * PART, PART), PART)
 
-    def kv_slot(array, head, part):
+    def slot(array, head, part):
+        if array == 2:
+            return qb.at[head, rows_of(part)]
         return kv.at[head, array, 1 + part // HALF, 1 + lax.rem(part // 4, 2), rows_of(lax.rem(part, 4))]
 
-    kv_in = (k_in, v_in)
+    sources = (k_in, v_in, q_in)
 
     loads = [pltpu.make_async_copy(count_in, count_s, small.at[0]),
              pltpu.make_async_copy(mask_in, mask_s, small.at[1])]
     for copy in loads:
         copy.start()
     for head in range(LOCAL_HEADS):
-        for array in range(2):
-            pltpu.make_async_copy(kv_in[array].at[:, columns(z, head)], kv_slot(array, head, z),
-                                  kv_recv.at[head, array]).start()
-        pltpu.make_async_copy(q_in.at[:, columns(z, head)], qb.at[head, rows_of(z)],
-                              q_recv.at[head]).start()
+        for array in range(3):
+            pltpu.make_async_copy(sources[array].at[:, columns(z, head)], slot(array, head, z),
+                                  in_recv.at[head, array]).start()
 
     for edge, at in ((~up, 0), (~down, 3)):
         @pl.when(edge)
@@ -141,25 +105,10 @@
         def body(step, carry):
             peer = lax.rem(z + ring(step), ULY)
             pltpu.make_async_remote_copy(
-                src_ref=kv_in[array].at[:, columns(peer, head)],
-                dst_ref=kv_slot(array, head, z),
+                src_ref=sources[array].at[:, columns(peer, head)],
+                dst_ref=slot(array, head, z),
                 send_sem=send_sem.at[array],
-                recv_sem=kv_recv.at[head, array],
-                device_id=(blk, peer),
-                device_id_type=MESH,
-            ).start()
-            return carry
-
-        lax.fori_loop(*steps, body, 0)
-
-    def scatter_queries(head, steps):
-        def body(step, carry):
-            peer = lax.rem(z + ring(step), ULY)
-            pltpu.make_async_remote_copy(
-                src_ref=q_in.at[:, columns(peer, head)],
-                dst_ref=qb.at[head, rows_of(z)],
-                send_sem=send_sem.at[2],
-                recv_sem=q_recv.at[head],
+                recv_sem=in_recv.at[head, array],
                 device_id=(blk, peer),
                 device_id_type=MESH,
             ).start()
@@ -186,7 +135,7 @@
                 ).start()
 
     def halo(array, head):
-        wait_bytes(qb.at[head], kv_recv.at[head, array])
+        wait_bytes(qb.at[head], in_recv.at[head, array])
         for a, b in others:
             @if_inside(a, b)
             def _():
@@ -251,11 +200,12 @@
         summed = jnp.dot(expo.astype(jnp.bfloat16), v, preferred_element_type=jnp.float32)
         ob[head, rows, :] = (summed / total).astype(jnp.bfloat16)
 
-    def give_back(head, steps, which):
+    def give_back(head, part_row):
         def body(step, carry):
-            peer = lax.rem(z + ring(step), ULY)
-
-            def send():
+            peer = part_row * HALF + step
+
+            @pl.when(peer != z)
+            def _():
                 pltpu.make_async_remote_copy(
                     src_ref=ob.at[head, rows_of(peer)],
                     dst_ref=out.at[:, columns(z, head)],
@@ -265,45 +215,54 @@
                     device_id_type=MESH,
                 ).start()
 
-            if which == 2:
-                send()
-            else:
-                pl.when((peer // HALF == half) == (which == 1))(send)
             return carry
 
-        lax.fori_loop(*steps, body, 0)
-
-    complete = set()
-    for step in SCHEDULE:
-        op, head, *rest = step
-        if op in ("k", "v"):
-            scatter("kv".index(op), head, *rest)
-        elif op == "q":
-            scatter_queries(head, *rest)
-        elif op in ("hk", "hv"):
-            halo("kv".index(op[1]), head)
-        elif op == "counts":
-            send_counts()
-        elif op == "bias":
+        lax.fori_loop(0, HALF, body, 0)
+
+    scatter(0, 0, ALL)
+    scatter(1, 0, ALL)
+    send_counts()
+    scatter(0, 1, ALL)
+    scatter(1, 1, ALL)
+    scatter(2, 0, ALL)
+    scatter(0, 2, ALL)
+    scatter(1, 2, ALL)
+    for steps in (FAR, NEAR):
+        for head in (1, 2):
+            scatter(2, head, steps)
+
+    def turn(i, carry):
+        @pl.when(i < LOCAL_HEADS)
+        def _():
+            lax.fori_loop(0, 2, lambda array, carry: halo(array, i), None)
+
+        @pl.when(i == 0)
+        def _():
             build_bias()
-        elif op == "c":
-            if head not in complete:
-                complete.add(head)
-                halo_arrived(0, head)
-                halo_arrived(1, head)
-                wait_bytes(qb.at[head], q_recv.at[head])
-            if rest[0] == 0:
-                compute(head, 1 - half)
-            else:
-                compute(head, half)
-                pltpu.make_async_copy(ob.at[head, rows_of(z)], out.at[:, columns(z, head)], out_recv).start()
-        elif op == "o":
-            give_back(head, *rest)
+
+        @pl.when(i > 0)
+        def _():
+            head = i - 1
+            lax.fori_loop(0, 2, lambda array, carry: halo_arrived(array, head), None)
+            wait_bytes(qb.at[head], in_recv.at[head, 2])
+            compute(head, 0)
+            give_back(head, 0)
+            compute(head, 1)
+            pltpu.make_async_copy(ob.at[head, rows_of(z)], out.at[:, columns(z, head)], out_recv).start()
+
+            @pl.when(head == 0)
+            def _():
+                give_back(head, 1)
+
+        return carry
+
+    lax.fori_loop(0, LOCAL_HEADS + 1, turn, 0)
+    give_back(1, 1)
+    give_back(2, 1)
 
     sent = pl.ds(0, LOCAL_HEADS * (ULY - 1) * HDIM)
-    for array in range(2):
-        wait_bytes(kv_in[array].at[:, sent], send_sem.at[array])
-    wait_bytes(q_in.at[:, sent], send_sem.at[2])
+    for array in range(3):
+        wait_bytes(sources[array].at[:, sent], send_sem.at[array])
     for a, b in others:
         @if_inside(a, b)
         def _():
@@ -331,7 +290,7 @@
             pltpu.SMEM((4,), jnp.int32),
             pltpu.SMEM((4, 27), jnp.int32),
             dma((2,)), dma((3,)), dma((9,)), dma((9,)), dma,
-            dma((heads, 2)), dma((heads,)), dma((heads, 2, 9)), dma((9,)), dma,
+            dma((heads, 3)), dma((heads, 2, 9)), dma((9,)), dma,
         ],
         compiler_params=pltpu.CompilerParams(
             collective_id=0, has_side_effects=True, vmem_limit_bytes=56 * 1024 * 1024),

time: 55.8 us -> 54.7 us (0.980)
  the two profiles are of different devices: /device:TPU:2 before, /device:TPU:4 now
where the time goes in v3:
time: 54.7 us; the launch traced here: 54.6 us
  Pallas kernels  53 us (97%)
  local copies, waits for them, and re-layouts  1.62 us (3%)
    pallas_call x1, Pallas kernels, on_device(): pl.pallas_call(kernel, out_shape=jax.ShapeDtypeStruct(queries.shape, quer...  53 us
    unnamed x1, local copies, waits for them, and re-layouts  1.62 us

profile of v3, /device:TPU:4, one launch (start us, length us, event | category | flops | bytes accessed | tf_op | source)
XLA Modules:
  0.0 54.6 jit_solution(5984524366441797809)
XLA Ops:
  0.0 53.0 %shard_map.55 = bf16[16,6144]{1,0:T(8,128)(2,1)} custom-call(s32[4]{0:T(128)} %count_in.1, s32[4,27]{1,0:T(4,128)} %mask_in.1, bf16[16,6144]{1,0:T(8,128)(2,1)} %q_in.1, bf16[16,6144]{1,0:T(8,128)(2,1)} %k_in.1, bf16[16,6144]{1,0:T(8,128)(2,1)} %v_in.1), custom_call_target="tpu_custom_call" | custom-call | tf_op jit(solution)/shard_map/pallas_call | solution.py:279
  53.0 1.6 %copy.7 = bf16[16,6144]{1,0:T(8,128)(2,1)} copy(bf16[16,6144]{1,0:T(8,128)(2,1)} %shard_map.55) | data formatting | bytes 393216

commit v4 on v3

--- a/solution.py
+++ b/solution.py
@@ -20,6 +20,8 @@
 MESH = pl.DeviceIdType.MESH
 
 ALL, FAR, NEAR = (0, ULY - 1), (0, 7), (7, ULY - 1)
+
+
 def near(move):
     return pl.ds(1, 2) if move == 0 else pl.ds(2, 1) if move == 1 else pl.ds(1, 1)
 
@@ -38,6 +40,7 @@
     blk = lax.axis_index("blk")
     z = lax.axis_index("uly")
     half = z // HALF
+    core = lax.rem(blk, 2)
     row, col = blk // COLB, blk % COLB
 
     up, down = row > 0, row < ROWB - 1
@@ -245,20 +248,33 @@
             head = i - 1
             lax.fori_loop(0, 2, lambda array, carry: halo_arrived(array, head), None)
             wait_bytes(qb.at[head], in_recv.at[head, 2])
-            compute(head, 0)
-            give_back(head, 0)
-            compute(head, 1)
-            pltpu.make_async_copy(ob.at[head, rows_of(z)], out.at[:, columns(z, head)], out_recv).start()
-
-            @pl.when(head == 0)
-            def _():
-                give_back(head, 1)
+            first = jnp.where(head == 1, core, 0)
+
+            def attend(row):
+                compute(head, row)
+                give_back(head, row)
+
+            attend(first)
+            pl.when((head == 0) | ((head == 1) & (core == 1)))(lambda: attend(1 - first))
 
         return carry
 
     lax.fori_loop(0, LOCAL_HEADS + 1, turn, 0)
-    give_back(1, 1)
-    give_back(2, 1)
+
+    @pl.when(core == 0)
+    def _():
+        compute(1, 1)
+        give_back(1, 1)
+        compute(2, 1)
+        give_back(2, 1)
+
+    @pl.when(core == 1)
+    def _():
+        compute(2, 1)
+        give_back(2, 1)
+
+    for head in range(LOCAL_HEADS):
+        pltpu.make_async_copy(ob.at[head, rows_of(z)], out.at[:, columns(z, head)], out_recv).start()
 
     sent = pl.ds(0, LOCAL_HEADS * (ULY - 1) * HDIM)
     for array in range(3):

time: 54.7 us -> 54.8 us (level)
  no operation moved by 1% of the time
where the time goes in v4:
time: 54.8 us; the launch traced here: 54.6 us
  Pallas kernels  53 us (97%)
  local copies, waits for them, and re-layouts  1.62 us (3%)
    pallas_call x1, Pallas kernels, on_device(): pl.pallas_call(kernel, out_shape=jax.ShapeDtypeStruct(queries.shape, quer...  53 us
    unnamed x1, local copies, waits for them, and re-layouts  1.62 us

profile of v4, /device:TPU:4, one launch (start us, length us, event | category | flops | bytes accessed | tf_op | source)
XLA Modules:
  0.0 54.6 jit_solution(18095146920482591302)
XLA Ops:
  0.0 53.0 %shard_map.55 = bf16[16,6144]{1,0:T(8,128)(2,1)} custom-call(s32[4]{0:T(128)} %count_in.1, s32[4,27]{1,0:T(4,128)} %mask_in.1, bf16[16,6144]{1,0:T(8,128)(2,1)} %q_in.1, bf16[16,6144]{1,0:T(8,128)(2,1)} %k_in.1, bf16[16,6144]{1,0:T(8,128)(2,1)} %v_in.1), custom_call_target="tpu_custom_call" | custom-call | tf_op jit(solution)/shard_map/pallas_call | solution.py:295
  53.0 1.6 %copy.7 = bf16[16,6144]{1,0:T(8,128)(2,1)} copy(bf16[16,6144]{1,0:T(8,128)(2,1)} %shard_map.55) | data formatting | bytes 393216

commit v5 on v4

--- a/solution.py
+++ b/solution.py
@@ -36,7 +36,7 @@
 
 def kernel(count_in, mask_in, q_in, k_in, v_in, out, kv, qb, ob, cnt, bias, count_s, mask_s,
            small, send_sem, halo_send, cnt_send, out_send,
-           in_recv, halo_recv, cnt_recv, out_recv):
+           in_recv, halo_recv, cnt_recv, out_recv, staged, stage_sem):
     blk = lax.axis_index("blk")
     z = lax.axis_index("uly")
     half = z // HALF
@@ -80,7 +80,11 @@
             return qb.at[head, rows_of(part)]
         return kv.at[head, array, 1 + part // HALF, 1 + lax.rem(part // 4, 2), rows_of(lax.rem(part, 4))]
 
-    sources = (k_in, v_in, q_in)
+    stages = [pltpu.make_async_copy(source, staged.at[array], stage_sem.at[array])
+              for array, source in enumerate((k_in, v_in, q_in))]
+    for copy in stages:
+        copy.start()
+    sources = [staged.at[array] for array in range(3)]
 
     loads = [pltpu.make_async_copy(count_in, count_s, small.at[0]),
              pltpu.make_async_copy(mask_in, mask_s, small.at[1])]
@@ -88,7 +92,7 @@
         copy.start()
     for head in range(LOCAL_HEADS):
         for array in range(3):
-            pltpu.make_async_copy(sources[array].at[:, columns(z, head)], slot(array, head, z),
+            pltpu.make_async_copy((k_in, v_in, q_in)[array].at[:, columns(z, head)], slot(array, head, z),
                                   in_recv.at[head, array]).start()
 
     for edge, at in ((~up, 0), (~down, 3)):
@@ -102,6 +106,8 @@
 
     across = 1 + left.astype(jnp.int32) + right.astype(jnp.int32)
     along = 1 + up.astype(jnp.int32) + down.astype(jnp.int32)
+    for copy in stages:
+        copy.wait()
     pl.semaphore_wait(barrier, ULY - 2 + across * along)
 
     def scatter(array, head, steps):
@@ -307,6 +313,7 @@
             pltpu.SMEM((4, 27), jnp.int32),
             dma((2,)), dma((3,)), dma((9,)), dma((9,)), dma,
             dma((heads, 3)), dma((heads, 2, 9)), dma((9,)), dma,
+            pltpu.VMEM((3,) + queries.shape, jnp.bfloat16), dma((3,)),
         ],
         compiler_params=pltpu.CompilerParams(
             collective_id=0, has_side_effects=True, vmem_limit_bytes=56 * 1024 * 1024),

time: 54.8 us -> 54.6 us (level)
  no operation moved by 1% of the time
where the time goes in v5:
time: 54.6 us; the launch traced here: 54.4 us
  Pallas kernels  52.8 us (97%)
  local copies, waits for them, and re-layouts  1.62 us (3%)
    pallas_call x1, Pallas kernels, on_device(): pl.pallas_call(kernel, out_shape=jax.ShapeDtypeStruct(queries.shape, quer...  52.8 us
    unnamed x1, local copies, waits for them, and re-layouts  1.62 us

profile of v5, /device:TPU:4, one launch (start us, length us, event | category | flops | bytes accessed | tf_op | source)
XLA Modules:
  0.0 54.4 jit_solution(6345251570361955939)
XLA Ops:
  0.0 52.8 %shard_map.55 = bf16[16,6144]{1,0:T(8,128)(2,1)} custom-call(s32[4]{0:T(128)} %count_in.1, s32[4,27]{1,0:T(4,128)} %mask_in.1, bf16[16,6144]{1,0:T(8,128)(2,1)} %q_in.1, bf16[16,6144]{1,0:T(8,128)(2,1)} %k_in.1, bf16[16,6144]{1,0:T(8,128)(2,1)} %v_in.1), custom_call_target="tpu_custom_call" | custom-call | tf_op jit(solution)/shard_map/pallas_call | solution.py:301
  52.8 1.6 %copy.7 = bf16[16,6144]{1,0:T(8,128)(2,1)} copy(bf16[16,6144]{1,0:T(8,128)(2,1)} %shard_map.55) | data formatting | bytes 393216

commit v6 on v5

--- a/solution.py
+++ b/solution.py
@@ -209,7 +209,7 @@
         summed = jnp.dot(expo.astype(jnp.bfloat16), v, preferred_element_type=jnp.float32)
         ob[head, rows, :] = (summed / total).astype(jnp.bfloat16)
 
-    def give_back(head, part_row):
+    def give_back(head, part_row, first=0, last=HALF):
         def body(step, carry):
             peer = part_row * HALF + step
 
@@ -226,7 +226,7 @@
 
             return carry
 
-        lax.fori_loop(0, HALF, body, 0)
+        lax.fori_loop(first, last, body, 0)
 
     scatter(0, 0, ALL)
     scatter(1, 0, ALL)
@@ -256,9 +256,11 @@
             wait_bytes(qb.at[head], in_recv.at[head, 2])
             first = jnp.where(head == 1, core, 0)
 
+            few = jnp.where((head == 1) & (core == 0), 3, HALF)
+
             def attend(row):
                 compute(head, row)
-                give_back(head, row)
+                give_back(head, row, 0, few)
 
             attend(first)
             pl.when((head == 0) | ((head == 1) & (core == 1)))(lambda: attend(1 - first))
@@ -269,6 +271,7 @@
 
     @pl.when(core == 0)
     def _():
+        give_back(1, 0, 3, HALF)
         compute(1, 1)
         give_back(1, 1)
         compute(2, 1)

time: 54.6 us -> 54.6 us (level)
  no operation moved by 1% of the time
where the time goes in v6:
time: 54.6 us; the launch traced here: 54.5 us
  Pallas kernels  52.8 us (97%)
  local copies, waits for them, and re-layouts  1.62 us (3%)
    pallas_call x1, Pallas kernels, on_device(): pl.pallas_call(kernel, out_shape=jax.ShapeDtypeStruct(queries.shape, quer...  52.8 us
    unnamed x1, local copies, waits for them, and re-layouts  1.62 us

profile of v6, /device:TPU:4, one launch (start us, length us, event | category | flops | bytes accessed | tf_op | source)
XLA Modules:
  0.0 54.5 jit_solution(16095709582419361977)
XLA Ops:
  0.0 52.8 %shard_map.55 = bf16[16,6144]{1,0:T(8,128)(2,1)} custom-call(s32[4]{0:T(128)} %count_in.1, s32[4,27]{1,0:T(4,128)} %mask_in.1, bf16[16,6144]{1,0:T(8,128)(2,1)} %q_in.1, bf16[16,6144]{1,0:T(8,128)(2,1)} %k_in.1, bf16[16,6144]{1,0:T(8,128)(2,1)} %v_in.1), custom_call_target="tpu_custom_call" | custom-call | tf_op jit(solution)/shard_map/pallas_call | solution.py:304
  52.9 1.6 %copy.7 = bf16[16,6144]{1,0:T(8,128)(2,1)} copy(bf16[16,6144]{1,0:T(8,128)(2,1)} %shard_map.55) | data formatting | bytes 393216
